TPU v7x, 1024 devices: a whole 4x4x32 slice. The times are simulated.
1024 devices in a mesh: leaf: 64 (over z, x_hi), panel: 16 (over y, x_lo, core).
Axes of the slice: x: 4 (x_hi: 2, x_lo: 2; x = x_hi * 2 + x_lo), y: 4, z: 32, core: 2. Of those that a mesh axis runs over, the one named last changes fastest.
Arguments:
- coupling: bfloat16 [64, 4096, 2048], P('leaf', 'panel'), may hold values from -6 to 6
- modes: bfloat16 [64, 2048, 256], P('leaf'), may hold values from -0.125 to 0.125
- eigvals: float32 [64, 256], P('leaf'), may hold values from 16 to 256
- sep_stiffness: bfloat16 [64, 4096, 2048], P('leaf', 'panel'), may hold values from -6 to 6
Outputs:
- reduced: bfloat16 [64, 4096, 2048], P('leaf', 'panel')
All inputs are finite; a program needn't handle non-finite values.
Results may differ from a plain program's by a relative error of at most 0.0042.
Values may be sent and summed in bfloat16 or wider, within the bound.
No kernel may reach another device: no remote copies, remote signals or barrier semaphores. Data moves between devices by JAX's collectives and lax.ppermute only.
A program may use at most 32 MiB of HBM per device.

v0:
```python
import jax
import jax.numpy as jnp
from jax import lax
from jax.sharding import PartitionSpec as P


def from_partner(value, axis, bit):
    mask = 2**bit
    pairs = [(source, source ^ mask) for source in range(lax.axis_size(axis))]
    return lax.ppermute(value, axis, pairs)


def shards(coupling, modes, eigvals, sep_stiffness):
    projected = jnp.dot(coupling[0], modes[0], preferred_element_type=jnp.float32)
    scaled = (projected * lax.rsqrt(eigvals[0])[None, :]).astype(jnp.bfloat16)
    half_cols = sep_stiffness.shape[2]
    parity = lax.axis_index("leaf") % 2
    sibling = from_partner(scaled, "leaf", 0)
    rows_both = jnp.concatenate([scaled, sibling], axis=1)
    gathered = lax.all_gather(rows_both, "panel", axis=0, tiled=True)
    columns = lax.dynamic_slice_in_dim(gathered, parity * half_cols, half_cols, 0)
    congruence = lax.dot_general(
        rows_both, columns, (((1,), (1,)), ((), ())), preferred_element_type=jnp.float32
    )
    reduced = sep_stiffness[0].astype(jnp.float32) - congruence
    return reduced.astype(jnp.bfloat16)[None]


def solution(mesh):
    placed = (
        P("leaf", "panel", None),
        P("leaf", None, None),
        P("leaf", None),
        P("leaf", "panel", None),
    )
    return jax.shard_map(
        shards, mesh=mesh, in_specs=placed, out_specs=P("leaf", "panel", None), check_vma=False
    )
```

profile of v0, /device:TPU:1, one launch (start us, length us, event | category | flops | bytes accessed | tf_op | source)
XLA Modules:
  0.0 101.8 jit_solution(5833367758793714222)
XLA Ops:
  6.5 0.0 copy-start
  6.5 0.0 copy-start.1
  6.5 0.0 all-gather.2.cloned.1.call-start
  6.5 0.8 rsqrt.4
  7.4 0.4 copy-done
  7.8 1.8 %fusion.3 = bf16[256,256]{0,1:T(8,128)(2,1)S(1)} fusion(bf16[1,2048,256]{2,1,0:T(8,128)(2,1)S(1)} %copy-done, bf16[1,256,2048]{2,1,0:T(8,128)(2,1)} %param.4, f32[256]{0:T(256)S(1)} %bitcast.12), kind=kOutput, calls=%fused_computation.5 | convolution fusion | flops 268566528 | bytes 2229248 | tf_op jit(solution)/shard_map/dot_general | solution.py:14
  9.6 5.5 %collective-permute-start = (bf16[256,256]{0,1:T(8,128)(2,1)S(1)}, bf16[256,256]{0,1:T(8,128)(2,1)S(1)}, u32[]{:S(2)}, u32[]{:S(2)}) collective-permute-start(bf16[256,256]{0,1:T(8,128)(2,1)S(1)} %fusion.3), channel_id=1, source_target_pairs={{0,16},{16,0},{32,48},{48,32},{64,80},{80,64},{96,112},{112,96},{1... | collective-permute-start | bytes 393224 | tf_op jit(solution)/shard_map/ppermute | solution.py:10
  15.1 2.3 %collective-permute-done = bf16[256,256]{0,1:T(8,128)(2,1)S(1)} collective-permute-done((bf16[256,256]{0,1:T(8,128)(2,1)S(1)}, bf16[256,256]{0,1:T(8,128)(2,1)S(1)}, u32[]{:S(2)}, u32[]{:S(2)}) %collective-permute-start) | collective-permute-done | bytes 131104 | tf_op jit(solution)/shard_map/ppermute | solution.py:10
  17.4 0.7 pad_maximum_fusion
  18.1 0.0 all-gather.2.cloned.1.call-update
  18.2 73.5 %all-gather.2.cloned.1.call-done = bf16[4096,512]{0,1:T(8,128)(2,1)} async-done(((bf16[256,512]{0,1:T(8,128)(2,1)}), bf16[4096,512]{0,1:T(8,128)(2,1)}) %all-gather.2.cloned.1.call-update) | async-done | bytes 4194320 | tf_op jit(solution)/shard_map/all_gather | solution.py:20
  91.7 0.0 copy-done.1
  91.7 3.3 %fusion.1 = bf16[1,256,2048]{2,1,0:T(8,128)(2,1)} fusion(bf16[4096,512]{0,1:T(8,128)(2,1)} %all-gather.2.cloned.1.call-done, s32[]{:T(128)S(6)} %select_n.11, bf16[1,256,2048]{2,1,0:T(8,128)(2,1)S(1)} %copy-done.1, bf16[256,256]{0,1:T(8,128)(2,1)S(1)} %collective-permute-done, bf16[256,256]{0,1:T(8,128)(2,1)S(1)} %fusion.3), kind=kOutput, calls=%fused_computation.2 | convolution fusion | flops 538968064 | bytes 4456452 | tf_op jit(solution)/shard_map/dot_general | solution.py:22
Async XLA Ops:
  6.5 1.2 %copy-start = (bf16[1,2048,256]{2,1,0:T(8,128)(2,1)S(1)}, bf16[1,2048,256]{2,1,0:T(8,128)(2,1)}, u32[]{:S(2)}) copy-start(bf16[1,2048,256]{2,1,0:T(8,128)(2,1)} %param.5) | copy-start | bytes 3145732
  6.5 85.1 %copy-start.1 = (bf16[1,256,2048]{2,1,0:T(8,128)(2,1)S(1)}, bf16[1,256,2048]{2,1,0:T(8,128)(2,1)}, u32[]{:S(2)}) copy-start(bf16[1,256,2048]{2,1,0:T(8,128)(2,1)} %param.7) | copy-start | bytes 3145732
  6.5 85.1 %all-gather.2.cloned.1.call-start = ((), (), s32[]{:S(2)}) async-start(), calls=%async_computation | async-start | bytes 4456448 | tf_op jit(solution)/shard_map/all_gather | solution.py:20
  9.6 7.8 %collective-permute-start = (bf16[256,256]{0,1:T(8,128)(2,1)S(1)}, bf16[256,256]{0,1:T(8,128)(2,1)S(1)}, u32[]{:S(2)}, u32[]{:S(2)}) collective-permute-start(bf16[256,256]{0,1:T(8,128)(2,1)S(1)} %fusion.3), channel_id=1, source_target_pairs={{0,16},{16,0},{32,48},{48,32},{64,80},{80,64},{96,112},{112,96},{1... | collective-permute-start | bytes 393224 | tf_op jit(solution)/shard_map/ppermute | solution.py:10
Sparse Core Ops, SparseCore 0:
  18.3 73.3 all-gather.1
where the time goes:
time: 102 us
  waiting for transfers between devices  75.9 us (74%)
  between operations  13.4 us (13%)
  starting transfers between devices  5.48 us (5%)
  matrix products  5.07 us (5%)
  local copies, waits for them, and re-layouts  1.24 us (1%)
    all_gather x1, waiting for transfers between devices, shards(): gathered = lax.all_gather(rows_both, 'panel', axis=0, tiled=True)  73.5 us
    ppermute x1, starting transfers between devices, from_partner(): return lax.ppermute(value, axis, pairs)  5.48 us
    dot_general x1, matrix products, shards(): lax.dot_general(rows_both, columns, (((1,), (1,)), ((), ())), preferred_e...  3.29 us
    ppermute x1, waiting for transfers between devices, from_partner(): return lax.ppermute(value, axis, pairs)  2.34 us
  transfers between devices with their start and end apart: 2, of which 2 were waited for; matrix products, arithmetic and copies ran while one was open for 0% of the time, Pallas kernels for 0%

commit v1 on v0

v1 whole, which is shorter than its diff:
```python
import functools

import jax
import jax.numpy as jnp
from jax import lax
from jax.experimental import pallas as pl
from jax.experimental.pallas import tpu as pltpu
from jax.sharding import PartitionSpec as P

AXES = ("leaf", "panel")
PANELS = 16
VMEM = pl.BlockSpec(memory_space=pltpu.VMEM)
HBM = pl.BlockSpec(memory_space=pltpu.HBM)


def pairs(move):
    found = []
    for parent in range(lax.axis_size("leaf") // 2):
        for bit in range(2):
            for panel in range(PANELS):
                target = move(bit, panel)
                if target is not None:
                    found.append((
                        (2 * parent + bit) * PANELS + panel,
                        (2 * parent + target[0]) * PANELS + target[1],
                    ))
    return found


def to_sibling(bit, panel):
    return (1 - bit, panel)


def to_far_rows(bit, panel):
    return (bit, panel ^ 12) if panel // 8 == bit else None


def to_core(bit, panel):
    return (bit, panel ^ 1)


def project_kernel(parts, coupling, modes, eigvals, scaled, a, b, sems):
    depth = a.shape[1] // parts
    copies = []
    for k in range(parts):
        cut = pl.ds(k * depth, depth)
        copies.append((
            pltpu.make_async_copy(coupling.at[0, :, cut], a.at[:, cut], sems.at[0, k]),
            pltpu.make_async_copy(modes.at[0, cut, :], b.at[cut, :], sems.at[1, k]),
        ))
    for pair in copies:
        for copy in pair:
            copy.start()
    total = jnp.zeros(scaled.shape, jnp.float32)
    for k, pair in enumerate(copies):
        for copy in pair:
            copy.wait()
        total += jnp.dot(
            a[:, k * depth : (k + 1) * depth],
            b[k * depth : (k + 1) * depth, :],
            preferred_element_type=jnp.float32,
        )
    scaled[...] = (total * lax.rsqrt(eigvals[...])).astype(jnp.bfloat16)


def project(coupling, modes, eigvals):
    rows, depth, columns = coupling.shape[1], coupling.shape[2], modes.shape[2]
    parts = 4
    return pl.pallas_call(
        functools.partial(project_kernel, parts),
        out_shape=jax.ShapeDtypeStruct((rows, columns), jnp.bfloat16),
        in_specs=[HBM, HBM, VMEM],
        out_specs=VMEM,
        scratch_shapes=[
            pltpu.VMEM((rows, depth), jnp.bfloat16),
            pltpu.VMEM((depth, columns), jnp.bfloat16),
            pltpu.SemaphoreType.DMA((2, parts)),
        ],
        compiler_params=pltpu.CompilerParams(vmem_limit_bytes=60 * 2**20),
        name="project",
    )(coupling, modes, eigvals)


def update_kernel(other_core, own, sibling, pieces, stiffness, so_far, out, held, made, in_sems, out_sems):
    del so_far
    bit = lax.axis_index("leaf") % 2
    core = lax.axis_index("panel") % 2
    core = 1 - core if other_core else core
    width = own.shape[0]
    loads, stores = [], []
    for n in range(4):
        cut = pl.ds(pl.multiple_of((2 * n + core) * width, width), width)
        loads.append(pltpu.make_async_copy(stiffness.at[0, :, cut], held.at[n], in_sems.at[n]))
        stores.append(pltpu.make_async_copy(made.at[n], out.at[0, :, cut], out_sems.at[n]))
    for copy in loads:
        copy.start()
    for n in range(4):
        ours = pieces[(1 - bit) * 4 + (n ^ 2)]
        others = pieces[bit * 4 + n]
        block = lax.dot_general(
            own[...], ours, (((1,), (1,)), ((), ())), preferred_element_type=jnp.float32
        ) + lax.dot_general(
            sibling[...], others, (((1,), (1,)), ((), ())), preferred_element_type=jnp.float32
        )
        loads[n].wait()
        made[n] = (held[n].astype(jnp.float32) - block).astype(jnp.bfloat16)
        stores[n].start()
    for copy in stores:
        copy.wait()


def update(other_core, own, sibling, pieces, stiffness, so_far):
    rows = own.shape[0]
    first = so_far is None
    kernel = functools.partial(update_kernel, other_core)
    if first:
        kernel = lambda own, sibling, pieces, stiffness, *rest: update_kernel(
            other_core, own, sibling, pieces, stiffness, None, *rest
        )
    return pl.pallas_call(
        kernel,
        out_shape=jax.ShapeDtypeStruct(stiffness.shape, stiffness.dtype),
        in_specs=[VMEM, VMEM, VMEM, HBM] + ([] if first else [HBM]),
        out_specs=HBM,
        scratch_shapes=[
            pltpu.VMEM((4, rows, rows), jnp.bfloat16),
            pltpu.VMEM((4, rows, rows), jnp.bfloat16),
            pltpu.SemaphoreType.DMA((4,)),
            pltpu.SemaphoreType.DMA((4,)),
        ],
        input_output_aliases={} if first else {4: 0},
        compiler_params=pltpu.CompilerParams(vmem_limit_bytes=16 * 2**20),
        cost_estimate=pl.CostEstimate(
            flops=2 * rows * 2 * rows * 4 * rows, bytes_accessed=6 * 2**20, transcendentals=0
        ),
        name="update_other" if other_core else "update_own",
    )(own, sibling, pieces, stiffness, *([] if first else [so_far]))


def shards(coupling, modes, eigvals, sep_stiffness):
    scaled = project(coupling, modes, eigvals)
    bit = lax.axis_index("leaf") % 2
    here = lax.axis_index("panel") // 8 == bit

    sibling = lax.ppermute(scaled, AXES, pairs(to_sibling))
    handed = lax.ppermute(scaled, AXES, pairs(to_far_rows))
    held = jnp.where(here, sibling, handed)
    groups = [list(range(core, PANELS, 2)) for core in range(2)]
    sent = jnp.broadcast_to(held[None], (8,) + held.shape)
    mine = lax.all_to_all(sent, "panel", 0, 0, axis_index_groups=groups)
    theirs = lax.ppermute(mine, AXES, pairs(to_core))
    half = update(False, scaled, sibling, mine, sep_stiffness, None)
    return update(True, scaled, sibling, theirs, sep_stiffness, half)


def solution(mesh):
    placed = (
        P("leaf", "panel", None),
        P("leaf", None, None),
        P("leaf", None),
        P("leaf", "panel", None),
    )
    return jax.shard_map(
        shards, mesh=mesh, in_specs=placed, out_specs=P("leaf", "panel", None), check_vma=False
    )
```

time: 102 us -> 51.3 us (0.50)
  waiting for transfers between devices: 75.9 us -> 2.32 us
  starting transfers between devices: 5.48 us -> 26.2 us
  blocking collectives: 0 us -> 14.6 us
  between operations: 13.4 us -> 0.12 us
  Pallas kernels: 0 us -> 7.69 us
  matrix products: 5.07 us -> 0 us
  local copies, waits for them, and re-layouts: 1.24 us -> 0.08 us
    all_gather x1 -> x0, waiting for transfers between devices: 73.5 us -> none  [shards(): gathered = lax.all_gather(rows_both, 'panel', axis=0, tiled=True)]
    ppermute x1 -> x3, starting transfers between devices: 5.48 us -> 26.2 us  [the longest x1 16.1 us: shards(): theirs = lax.ppermute(mine, AXES, pairs(to_core))]
    all_to_all x0 -> x1, blocking collectives: none -> 14.6 us  [shards(): mine = lax.all_to_all(sent, 'panel', 0, 0, axis_index_groups=groups)]
    pallas_call x0 -> x3, Pallas kernels: none -> 7.69 us  [the longest x2 4.22 us: update(): pl.pallas_call(kernel, out_shape=jax.ShapeDtypeStruct(stiffness.shape, st...]
    dot_general x2 -> x0, matrix products: 5.07 us -> none  [the longest x1 3.29 us: shards(): lax.dot_general(rows_both, columns, (((1,), (1,)), ((), ())), preferred_e...]
    ppermute x1 -> x3, waiting for transfers between devices: 2.34 us -> 2.32 us  [the longest x1 2.21 us: shards(): handed = lax.ppermute(scaled, AXES, pairs(to_far_rows))]
  transfers between devices with their start and end apart: 2 -> 3, of which waited for: 2 -> 2; matrix products, arithmetic and copies ran while one was open for 0% -> 0% of each run, Pallas kernels for 0% -> 4%
where the time goes in v1:
time: 51.3 us; the launch traced here: 51 us
  starting transfers between devices  26.2 us (51%)
  blocking collectives  14.6 us (28%)
  Pallas kernels  7.69 us (15%)
  waiting for transfers between devices  2.32 us (5%)
    ppermute x1, starting transfers between devices, shards(): theirs = lax.ppermute(mine, AXES, pairs(to_core))  16.1 us
    all_to_all x1, blocking collectives, shards(): mine = lax.all_to_all(sent, 'panel', 0, 0, axis_index_groups=groups)  14.6 us
    ppermute x1, starting transfers between devices, shards(): sibling = lax.ppermute(scaled, AXES, pairs(to_sibling))  5.48 us
    ppermute x1, starting transfers between devices, shards(): handed = lax.ppermute(scaled, AXES, pairs(to_far_rows))  4.65 us
    pallas_call x2, Pallas kernels, update(): pl.pallas_call(kernel, out_shape=jax.ShapeDtypeStruct(stiffness.shape, st...  4.22 us
    pallas_call x1, Pallas kernels, project(): pl.pallas_call(functools.partial(project_kernel, parts), out_shape=jax.Sh...  3.47 us
    ppermute x1, waiting for transfers between devices, shards(): handed = lax.ppermute(scaled, AXES, pairs(to_far_rows))  2.21 us
  transfers between devices with their start and end apart: 3, of which 2 were waited for; matrix products, arithmetic and copies ran while one was open for 0% of the time, Pallas kernels for 4%

profile of v1, /device:TPU:1, one launch (start us, length us, event | category | flops | bytes accessed | tf_op | source)
XLA Modules:
  0.0 51.0 jit_solution(8408942438787271834)
XLA Ops:
  0.0 3.5 %project.1.own = bf16[256,256]{1,0:T(8,128)(2,1)} custom-call(bf16[1,256,2048]{2,1,0:T(8,128)(2,1)} %coupling.1, bf16[1,2048,256]{2,1,0:T(8,128)(2,1)} %modes.1, f32[1,256]{1,0:T(1,128)} %eigvals.1), custom_call_target="tpu_custom_call" | custom-call | tf_op jit(solution)/shard_map/project/pallas_call | solution.py:69
  3.5 5.5 %collective-permute-start = (bf16[256,256]{1,0:T(8,128)(2,1)}, bf16[256,256]{1,0:T(8,128)(2,1)S(1)}, u32[]{:S(2)}, u32[]{:S(2)}) collective-permute-start(bf16[256,256]{1,0:T(8,128)(2,1)} %project.1.own), channel_id=1, source_target_pairs={{0,16},{1,17},{2,18},{3,19},{4,20},{5,21},{6,22},{7,23},{8,24},{9,... | collective-permute-start | bytes 393224 | tf_op jit(solution)/shard_map/ppermute | solution.py:145
  9.0 4.6 %collective-permute-start.1 = (bf16[256,256]{1,0:T(8,128)(2,1)}, bf16[256,256]{1,0:T(8,128)(2,1)S(1)}, u32[]{:S(2)}, u32[]{:S(2)}) collective-permute-start(bf16[256,256]{1,0:T(8,128)(2,1)} %project.1.own), channel_id=1, source_target_pairs={{0,12},{1,13},{2,14},{3,15},{4,8},{5,9},{6,10},{7,11},{24,20},{25,... | collective-permute-start | bytes 393224 | tf_op jit(solution)/shard_map/ppermute | solution.py:146
  13.6 0.0 collective-permute-done.sibling
  13.7 2.2 %collective-permute-done.1 = bf16[256,256]{1,0:T(8,128)(2,1)S(1)} collective-permute-done((bf16[256,256]{1,0:T(8,128)(2,1)}, bf16[256,256]{1,0:T(8,128)(2,1)S(1)}, u32[]{:S(2)}, u32[]{:S(2)}) %collective-permute-start.1) | collective-permute-done | bytes 131104 | tf_op jit(solution)/shard_map/ppermute | solution.py:146
  15.9 0.1 broadcast_in_dim.2
  16.0 0.0 copy-start
  16.0 0.0 copy-start.1
  16.0 14.6 %all_to_all.5.pieces = bf16[8,256,256]{2,1,0:T(8,128)(2,1)S(1)} all-to-all(bf16[8,256,256]{2,1,0:T(8,128)(2,1)S(1)} %broadcast_in_dim.2), channel_id=1, replica_groups={{0,2,4,6,8,10,12,14},{1,3,5,7,9,11,13,15},{16,18,20,22,24,26,28,30},{17..., dimensions={0} | all-to-all | bytes 2097152 | tf_op jit(solution)/shard_map/all_to_all | solution.py:150
  30.5 16.1 %collective-permute-start.2 = (bf16[8,256,256]{2,1,0:T(8,128)(2,1)S(1)}, bf16[8,256,256]{2,1,0:T(8,128)(2,1)S(1)}, u32[]{:S(2)}, u32[]{:S(2)}) collective-permute-start(bf16[8,256,256]{2,1,0:T(8,128)(2,1)S(1)} %all_to_all.5.pieces), channel_id=1, source_target_pairs={{0,1},{1,0},{2,3},{3,2},{4,5},{5,4},{6,7},{7,6},{8,9},{9,8},{10,11... | collective-permute-start | bytes 3145736 | tf_op jit(solution)/shard_map/ppermute | solution.py:151
  46.6 0.0 copy-done
  46.6 0.0 copy-done.1
  46.7 2.1 %update_own.1.so_far = bf16[1,256,2048]{2,1,0:T(8,128)(2,1)} custom-call(bf16[256,256]{1,0:T(8,128)(2,1)S(1)} %copy-done.1, bf16[256,256]{1,0:T(8,128)(2,1)S(1)} %collective-permute-done.sibling, bf16[8,256,256]{2,1,0:T(8,128)(2,1)S(1)} %all_to_all.5.pieces, bf16[1,256,2048]{2,1,0:T(8,128)(2,1)S(1)} %copy-done), custom_call_target="tpu_custom_call" | custom-call | flops 268435456 | bytes 6291456 | tf_op jit(solution)/shard_map/update_own/pallas_call | solution.py:120
  48.8 0.1 collective-permute-done.2.pieces
  48.9 2.1 %update_other.1 = bf16[1,256,2048]{2,1,0:T(8,128)(2,1)} custom-call(bf16[256,256]{1,0:T(8,128)(2,1)S(1)} %copy-done.1, bf16[256,256]{1,0:T(8,128)(2,1)S(1)} %collective-permute-done.sibling, bf16[8,256,256]{2,1,0:T(8,128)(2,1)S(1)} %collective-permute-done.2.pieces, bf16[1,256,2048]{2,1,0:T(8,128)(2,1)S(1)} %copy-done, ...), custom_call_target="tpu_custom_call", output_to_operand_aliasing={{}: (4, {})} | custom-call | flops 268435456 | bytes 6291456 | tf_op jit(solution)/shard_map/update_other/pallas_call | solution.py:120
  (1 shorter events, 0.0 us)
Async XLA Ops:
  3.5 10.2 %collective-permute-start = (bf16[256,256]{1,0:T(8,128)(2,1)}, bf16[256,256]{1,0:T(8,128)(2,1)S(1)}, u32[]{:S(2)}, u32[]{:S(2)}) collective-permute-start(bf16[256,256]{1,0:T(8,128)(2,1)} %project.1.own), channel_id=1, source_target_pairs={{0,16},{1,17},{2,18},{3,19},{4,20},{5,21},{6,22},{7,23},{8,24},{9,... | collective-permute-start | bytes 393224 | tf_op jit(solution)/shard_map/ppermute | solution.py:145
  9.0 6.9 %collective-permute-start.1 = (bf16[256,256]{1,0:T(8,128)(2,1)}, bf16[256,256]{1,0:T(8,128)(2,1)S(1)}, u32[]{:S(2)}, u32[]{:S(2)}) collective-permute-start(bf16[256,256]{1,0:T(8,128)(2,1)} %project.1.own), channel_id=1, source_target_pairs={{0,12},{1,13},{2,14},{3,15},{4,8},{5,9},{6,10},{7,11},{24,20},{25,... | collective-permute-start | bytes 393224 | tf_op jit(solution)/shard_map/ppermute | solution.py:146
  16.0 30.7 %copy-start = (bf16[1,256,2048]{2,1,0:T(8,128)(2,1)S(1)}, bf16[1,256,2048]{2,1,0:T(8,128)(2,1)}, u32[]{:S(2)}) copy-start(bf16[1,256,2048]{2,1,0:T(8,128)(2,1)} %stiffness.3) | copy-start | bytes 3145732
  16.0 30.7 %copy-start.1 = (bf16[256,256]{1,0:T(8,128)(2,1)S(1)}, bf16[256,256]{1,0:T(8,128)(2,1)}, u32[]{:S(2)}) copy-start(bf16[256,256]{1,0:T(8,128)(2,1)} %project.1.own) | copy-start | bytes 393220
  30.5 18.4 %collective-permute-start.2 = (bf16[8,256,256]{2,1,0:T(8,128)(2,1)S(1)}, bf16[8,256,256]{2,1,0:T(8,128)(2,1)S(1)}, u32[]{:S(2)}, u32[]{:S(2)}) collective-permute-start(bf16[8,256,256]{2,1,0:T(8,128)(2,1)S(1)} %all_to_all.5.pieces), channel_id=1, source_target_pairs={{0,1},{1,0},{2,3},{3,2},{4,5},{5,4},{6,7},{7,6},{8,9},{9,8},{10,11... | collective-permute-start | bytes 3145736 | tf_op jit(solution)/shard_map/ppermute | solution.py:151

commit v2 on v1

v2 whole, which is shorter than its diff:
```python
import functools

import jax
import jax.numpy as jnp
from jax import lax
from jax.experimental import pallas as pl
from jax.experimental.pallas import tpu as pltpu
from jax.sharding import PartitionSpec as P

AXES = ("leaf", "panel")
PANELS = 16
VMEM = pl.BlockSpec(memory_space=pltpu.VMEM)
HBM = pl.BlockSpec(memory_space=pltpu.HBM)


def pairs(move):
    found = []
    for parent in range(lax.axis_size("leaf") // 2):
        for bit in range(2):
            for panel in range(PANELS):
                target = move(bit, panel)
                if target is not None:
                    found.append((
                        (2 * parent + bit) * PANELS + panel,
                        (2 * parent + target[0]) * PANELS + target[1],
                    ))
    return found


def across(bit, panel):
    return None if panel // 8 == bit else (1 - bit, panel ^ 14)


def to_sibling(bit, panel):
    return (1 - bit, panel) if panel // 8 == bit else None


def to_core(bit, panel):
    return (bit, panel ^ 1)


def project_kernel(parts, coupling, modes, eigvals, scaled, a, b, e, sems, last):
    depth = a.shape[1] // parts
    copies = []
    for k in range(parts):
        cut = pl.ds(k * depth, depth)
        copies.append((
            pltpu.make_async_copy(coupling.at[0, :, cut], a.at[:, cut], sems.at[0, k]),
            pltpu.make_async_copy(modes.at[0, cut, :], b.at[cut, :], sems.at[1, k]),
        ))
    for pair in copies:
        for copy in pair:
            copy.start()
    gains = pltpu.make_async_copy(eigvals, e, last)
    gains.start()
    total = jnp.zeros(scaled.shape, jnp.float32)
    for k, pair in enumerate(copies):
        for copy in pair:
            copy.wait()
        total += jnp.dot(
            a[:, k * depth : (k + 1) * depth],
            b[k * depth : (k + 1) * depth, :],
            preferred_element_type=jnp.float32,
        )
    gains.wait()
    scaled[...] = (total * lax.rsqrt(e[...])).astype(jnp.bfloat16)


def project(coupling, modes, eigvals):
    rows, depth, columns = coupling.shape[1], coupling.shape[2], modes.shape[2]
    parts = 4
    return pl.pallas_call(
        functools.partial(project_kernel, parts),
        out_shape=jax.ShapeDtypeStruct((rows, columns), jnp.bfloat16),
        in_specs=[HBM, HBM, HBM],
        out_specs=VMEM,
        scratch_shapes=[
            pltpu.VMEM((rows, depth), jnp.bfloat16),
            pltpu.VMEM((depth, columns), jnp.bfloat16),
            pltpu.VMEM((1, columns), jnp.float32),
            pltpu.SemaphoreType.DMA((2, parts)),
            pltpu.SemaphoreType.DMA,
        ],
        compiler_params=pltpu.CompilerParams(vmem_limit_bytes=53 * 2**20),
        name="project",
    )(coupling, modes, eigvals)


def update_kernel(other_core, own, sibling, mine, pieces, stiffness, out, made, sems):
    bit, panel = lax.axis_index("leaf") % 2, lax.axis_index("panel")
    core = 1 - panel % 2 if other_core else panel % 2
    here = panel // 8 == bit
    width = own.shape[0]
    partner = jnp.where(here, mine[(1 - bit) * 4 + 3 - (panel % 8) // 2], sibling[...])
    stores = []
    for n in range(4):
        cut = pl.ds(pl.multiple_of((2 * n + core) * width, width), width)
        block = lax.dot_general(
            own[...], pieces[bit * 4 + n], (((1,), (1,)), ((), ())), preferred_element_type=jnp.float32
        ) + lax.dot_general(
            partner,
            pieces[(1 - bit) * 4 + 3 - n],
            (((1,), (1,)), ((), ())),
            preferred_element_type=jnp.float32,
        )
        made[n] = (stiffness[0, :, cut].astype(jnp.float32) - block).astype(jnp.bfloat16)
        stores.append(pltpu.make_async_copy(made.at[n], out.at[0, :, cut], sems.at[n]))
        stores[n].start()
    for copy in stores:
        copy.wait()


def update_own_kernel(own, sibling, mine, stiffness, *rest):
    update_kernel(False, own, sibling, mine, mine, stiffness, *rest)


def update_other_kernel(own, sibling, mine, theirs, stiffness, so_far, *rest):
    del so_far
    update_kernel(True, own, sibling, mine, theirs, stiffness, *rest)


def update(kernel, name, arrays, stiffness, so_far):
    rows = arrays[0].shape[0]
    before = [] if so_far is None else [so_far]
    count = len(arrays) + 1
    return pl.pallas_call(
        kernel,
        out_shape=jax.ShapeDtypeStruct(stiffness.shape, stiffness.dtype),
        in_specs=[VMEM] * count + [HBM] * len(before),
        out_specs=HBM,
        scratch_shapes=[
            pltpu.VMEM((4, rows, rows), jnp.bfloat16),
            pltpu.SemaphoreType.DMA((4,)),
        ],
        input_output_aliases={count: 0} if before else {},
        compiler_params=pltpu.CompilerParams(vmem_limit_bytes=16 * 2**20),
        cost_estimate=pl.CostEstimate(
            flops=2 * rows * 2 * rows * 4 * rows, bytes_accessed=2 * 2**20, transcendentals=0
        ),
        name=name,
    )(*arrays, stiffness, *before)


def shards(coupling, modes, eigvals, sep_stiffness):
    scaled = project(coupling, modes, eigvals)
    bit = lax.axis_index("leaf") % 2
    here = lax.axis_index("panel") // 8 == bit

    crossed = lax.ppermute(scaled, AXES, pairs(across))
    sibling = lax.ppermute(scaled, AXES, pairs(to_sibling))
    held = jnp.where(here, scaled, crossed)
    held, sibling = lax.optimization_barrier((held, sibling))
    groups = [list(range(core, PANELS, 2)) for core in range(2)]
    sent = jnp.broadcast_to(held[None], (8,) + held.shape)
    mine = lax.all_to_all(sent, "panel", 0, 0, axis_index_groups=groups)
    theirs = lax.ppermute(mine, AXES, pairs(to_core))
    half = update(update_own_kernel, "update_own", (scaled, sibling, mine), sep_stiffness, None)
    return update(update_other_kernel, "update_other", (scaled, sibling, mine, theirs), sep_stiffness, half)


def solution(mesh):
    placed = (
        P("leaf", "panel", None),
        P("leaf", None, None),
        P("leaf", None),
        P("leaf", "panel", None),
    )
    return jax.shard_map(
        shards, mesh=mesh, in_specs=placed, out_specs=P("leaf", "panel", None), check_vma=False
    )
```

time: 51.3 us -> 42.4 us (0.83)
  starting transfers between devices: 26.2 us -> 18.9 us
  Pallas kernels: 7.69 us -> 4.6 us
  local copies, waits for them, and re-layouts: 0.08 us -> 0.75 us
  waiting for transfers between devices: 2.32 us -> 2.89 us
    ppermute x1, starting transfers between devices: 16.1 us -> 8.75 us  [shards(): theirs = lax.ppermute(mine, AXES, pairs(to_core))]
    ppermute x1, starting transfers between devices: 4.65 us -> 0.67 us  [shards(): crossed = lax.ppermute(scaled, AXES, pairs(across))]
    ppermute x1, starting transfers between devices: 5.48 us -> 9.43 us  [shards(): sibling = lax.ppermute(scaled, AXES, pairs(to_sibling))]
    ppermute x1, waiting for transfers between devices: 2.21 us -> 0.01 us  [shards(): crossed = lax.ppermute(scaled, AXES, pairs(across))]
    ppermute x1, waiting for transfers between devices: 0.01 us -> 1.86 us  [shards(): sibling = lax.ppermute(scaled, AXES, pairs(to_sibling))]
    pallas_call x2, Pallas kernels: 4.22 us -> 2.43 us  [update(): pl.pallas_call(kernel, out_shape=jax.ShapeDtypeStruct(stiffness.shape, st...]
    pallas_call x1, Pallas kernels: 3.47 us -> 2.17 us  [project(): pl.pallas_call(functools.partial(project_kernel, parts), out_shape=jax.Sh...]
    ppermute x1, waiting for transfers between devices: 0.12 us -> 1.02 us  [shards(): theirs = lax.ppermute(mine, AXES, pairs(to_core))]
  transfers between devices with their start and end apart: 3 -> 3, of which waited for: 2 -> 2; matrix products, arithmetic and copies ran while one was open for 0% -> 0% of each run, Pallas kernels for 4% -> 3%
where the time goes in v2:
time: 42.4 us; the launch traced here: 42 us
  starting transfers between devices  18.9 us (45%)
  blocking collectives  14.8 us (35%)
  Pallas kernels  4.6 us (11%)
  waiting for transfers between devices  2.89 us (7%)
  local copies, waits for them, and re-layouts  0.75 us (2%)
    all_to_all x1, blocking collectives, shards(): mine = lax.all_to_all(sent, 'panel', 0, 0, axis_index_groups=groups)  14.8 us
    ppermute x1, starting transfers between devices, shards(): sibling = lax.ppermute(scaled, AXES, pairs(to_sibling))  9.43 us
    ppermute x1, starting transfers between devices, shards(): theirs = lax.ppermute(mine, AXES, pairs(to_core))  8.75 us
    pallas_call x2, Pallas kernels, update(): pl.pallas_call(kernel, out_shape=jax.ShapeDtypeStruct(stiffness.shape, st...  2.43 us
    pallas_call x1, Pallas kernels, project(): pl.pallas_call(functools.partial(project_kernel, parts), out_shape=jax.Sh...  2.17 us
    ppermute x1, waiting for transfers between devices, shards(): sibling = lax.ppermute(scaled, AXES, pairs(to_sibling))  1.86 us
    ppermute x1, waiting for transfers between devices, shards(): theirs = lax.ppermute(mine, AXES, pairs(to_core))  1.02 us
  transfers between devices with their start and end apart: 3, of which 2 were waited for; matrix products, arithmetic and copies ran while one was open for 0% of the time, Pallas kernels for 3%

profile of v2, /device:TPU:1, one launch (start us, length us, event | category | flops | bytes accessed | tf_op | source)
XLA Modules:
  0.0 42.0 jit_solution(8690049045230306043)
XLA Ops:
  0.0 0.0 copy-start.1
  0.0 0.7 %copy-done.1 = f32[1,256]{1,0:T(1,128)S(1)} copy-done((f32[1,256]{1,0:T(1,128)S(1)}, f32[1,256]{1,0:T(1,128)}, u32[]{:S(2)}) %copy-start.1) | copy-done | bytes 1048
  0.7 2.2 %project.1.own = bf16[256,256]{1,0:T(8,128)(2,1)S(1)} custom-call(bf16[1,256,2048]{2,1,0:T(8,128)(2,1)} %coupling.1, bf16[1,2048,256]{2,1,0:T(8,128)(2,1)} %modes.1, f32[1,256]{1,0:T(1,128)S(1)} %copy-done.1), custom_call_target="tpu_custom_call" | custom-call | tf_op jit(solution)/shard_map/project/pallas_call | solution.py:72
  2.9 0.7 %collective-permute-start = (bf16[256,256]{1,0:T(8,128)(2,1)S(1)}, bf16[256,256]{1,0:T(8,128)(2,1)S(1)}, u32[]{:S(2)}, u32[]{:S(2)}) collective-permute-start(bf16[256,256]{1,0:T(8,128)(2,1)S(1)} %project.1.own), channel_id=1, source_target_pairs={{8,22},{9,23},{10,20},{11,21},{12,18},{13,19},{14,16},{15,17},{16,... | collective-permute-start | bytes 393224 | tf_op jit(solution)/shard_map/ppermute | solution.py:149
  3.5 9.4 %collective-permute-start.1 = (bf16[256,256]{1,0:T(8,128)(2,1)S(1)}, bf16[256,256]{1,0:T(8,128)(2,1)S(1)}, u32[]{:S(2)}, u32[]{:S(2)}) collective-permute-start(bf16[256,256]{1,0:T(8,128)(2,1)S(1)} %project.1.own), channel_id=1, source_target_pairs={{0,16},{1,17},{2,18},{3,19},{4,20},{5,21},{6,22},{7,23},{24,8},{25... | collective-permute-start | bytes 393224 | tf_op jit(solution)/shard_map/ppermute | solution.py:150
  13.0 0.0 collective-permute-done
  13.0 1.9 %collective-permute-done.1.sibling = bf16[256,256]{1,0:T(8,128)(2,1)S(1)} collective-permute-done((bf16[256,256]{1,0:T(8,128)(2,1)S(1)}, bf16[256,256]{1,0:T(8,128)(2,1)S(1)}, u32[]{:S(2)}, u32[]{:S(2)}) %collective-permute-start.1) | collective-permute-done | bytes 131104 | tf_op jit(solution)/shard_map/ppermute | solution.py:150
  14.9 0.1 broadcast_in_dim.2
  15.0 0.0 copy-start
  15.0 14.8 %all_to_all.5.mine = bf16[8,256,256]{2,1,0:T(8,128)(2,1)S(1)} all-to-all(bf16[8,256,256]{2,1,0:T(8,128)(2,1)S(1)} %broadcast_in_dim.2), channel_id=1, replica_groups={{0,2,4,6,8,10,12,14},{1,3,5,7,9,11,13,15},{16,18,20,22,24,26,28,30},{17..., dimensions={0} | all-to-all | bytes 2097152 | tf_op jit(solution)/shard_map/all_to_all | solution.py:155
  29.8 8.8 %collective-permute-start.2 = (bf16[8,256,256]{2,1,0:T(8,128)(2,1)S(1)}, bf16[8,256,256]{2,1,0:T(8,128)(2,1)S(1)}, u32[]{:S(2)}, u32[]{:S(2)}) collective-permute-start(bf16[8,256,256]{2,1,0:T(8,128)(2,1)S(1)} %all_to_all.5.mine), channel_id=1, source_target_pairs={{0,1},{1,0},{2,3},{3,2},{4,5},{5,4},{6,7},{7,6},{8,9},{9,8},{10,11... | collective-permute-start | bytes 3145736 | tf_op jit(solution)/shard_map/ppermute | solution.py:156
  38.5 0.0 copy-done
  38.5 1.2 %update_own.1.so_far = bf16[1,256,2048]{2,1,0:T(8,128)(2,1)} custom-call(bf16[256,256]{1,0:T(8,128)(2,1)S(1)} %project.1.own, bf16[256,256]{1,0:T(8,128)(2,1)S(1)} %collective-permute-done.1.sibling, bf16[8,256,256]{2,1,0:T(8,128)(2,1)S(1)} %all_to_all.5.mine, bf16[1,256,2048]{2,1,0:T(8,128)(2,1)S(1)} %copy-done), custom_call_target="tpu_custom_call" | custom-call | flops 268435456 | bytes 2097152 | tf_op jit(solution)/shard_map/update_own/pallas_call | solution.py:126
  39.8 1.0 %collective-permute-done.2.theirs = bf16[8,256,256]{2,1,0:T(8,128)(2,1)S(1)} collective-permute-done((bf16[8,256,256]{2,1,0:T(8,128)(2,1)S(1)}, bf16[8,256,256]{2,1,0:T(8,128)(2,1)S(1)}, u32[]{:S(2)}, u32[]{:S(2)}) %collective-permute-start.2) | collective-permute-done | bytes 1048608 | tf_op jit(solution)/shard_map/ppermute | solution.py:156
  40.8 1.2 %update_other.1 = bf16[1,256,2048]{2,1,0:T(8,128)(2,1)} custom-call(bf16[256,256]{1,0:T(8,128)(2,1)S(1)} %project.1.own, bf16[256,256]{1,0:T(8,128)(2,1)S(1)} %collective-permute-done.1.sibling, bf16[8,256,256]{2,1,0:T(8,128)(2,1)S(1)} %all_to_all.5.mine, bf16[8,256,256]{2,1,0:T(8,128)(2,1)S(1)} %collective-permute-done.2.theirs, ...), custom_call_target="tpu_custom_call", output_to_operand_aliasing={{}: (5, {})} | custom-call | flops 268435456 | bytes 2097152 | tf_op jit(solution)/shard_map/update_other/pallas_call | solution.py:126
  (1 shorter events, 0.0 us)
Async XLA Ops:
  0.0 0.7 %copy-start.1 = (f32[1,256]{1,0:T(1,128)S(1)}, f32[1,256]{1,0:T(1,128)}, u32[]{:S(2)}) copy-start(f32[1,256]{1,0:T(1,128)} %eigvals.1) | copy-start | bytes 3076
  2.9 10.1 %collective-permute-start = (bf16[256,256]{1,0:T(8,128)(2,1)S(1)}, bf16[256,256]{1,0:T(8,128)(2,1)S(1)}, u32[]{:S(2)}, u32[]{:S(2)}) collective-permute-start(bf16[256,256]{1,0:T(8,128)(2,1)S(1)} %project.1.own), channel_id=1, source_target_pairs={{8,22},{9,23},{10,20},{11,21},{12,18},{13,19},{14,16},{15,17},{16,... | collective-permute-start | bytes 393224 | tf_op jit(solution)/shard_map/ppermute | solution.py:149
  3.5 11.4 %collective-permute-start.1 = (bf16[256,256]{1,0:T(8,128)(2,1)S(1)}, bf16[256,256]{1,0:T(8,128)(2,1)S(1)}, u32[]{:S(2)}, u32[]{:S(2)}) collective-permute-start(bf16[256,256]{1,0:T(8,128)(2,1)S(1)} %project.1.own), channel_id=1, source_target_pairs={{0,16},{1,17},{2,18},{3,19},{4,20},{5,21},{6,22},{7,23},{24,8},{25... | collective-permute-start | bytes 393224 | tf_op jit(solution)/shard_map/ppermute | solution.py:150
  15.0 23.6 %copy-start = (bf16[1,256,2048]{2,1,0:T(8,128)(2,1)S(1)}, bf16[1,256,2048]{2,1,0:T(8,128)(2,1)}, u32[]{:S(2)}) copy-start(bf16[1,256,2048]{2,1,0:T(8,128)(2,1)} %stiffness.3) | copy-start | bytes 3145732
  29.8 11.0 %collective-permute-start.2 = (bf16[8,256,256]{2,1,0:T(8,128)(2,1)S(1)}, bf16[8,256,256]{2,1,0:T(8,128)(2,1)S(1)}, u32[]{:S(2)}, u32[]{:S(2)}) collective-permute-start(bf16[8,256,256]{2,1,0:T(8,128)(2,1)S(1)} %all_to_all.5.mine), channel_id=1, source_target_pairs={{0,1},{1,0},{2,3},{3,2},{4,5},{5,4},{6,7},{7,6},{8,9},{9,8},{10,11... | collective-permute-start | bytes 3145736 | tf_op jit(solution)/shard_map/ppermute | solution.py:156

commit v3 on v2

--- a/solution.py
+++ b/solution.py
@@ -9,6 +9,7 @@
 
 AXES = ("leaf", "panel")
 PANELS = 16
+PROJECT_VMEM = 211 * 2**18
 VMEM = pl.BlockSpec(memory_space=pltpu.VMEM)
 HBM = pl.BlockSpec(memory_space=pltpu.HBM)
 
@@ -39,7 +40,7 @@
     return (bit, panel ^ 1)
 
 
-def project_kernel(parts, coupling, modes, eigvals, scaled, a, b, e, sems, last):
+def project_kernel(parts, coupling, modes, projected, a, b, sems):
     depth = a.shape[1] // parts
     copies = []
     for k in range(parts):
@@ -51,39 +52,35 @@
     for pair in copies:
         for copy in pair:
             copy.start()
-    gains = pltpu.make_async_copy(eigvals, e, last)
-    gains.start()
-    total = jnp.zeros(scaled.shape, jnp.float32)
+    total = None
     for k, pair in enumerate(copies):
         for copy in pair:
             copy.wait()
-        total += jnp.dot(
+        term = jnp.dot(
             a[:, k * depth : (k + 1) * depth],
             b[k * depth : (k + 1) * depth, :],
             preferred_element_type=jnp.float32,
         )
-    gains.wait()
-    scaled[...] = (total * lax.rsqrt(e[...])).astype(jnp.bfloat16)
+        total = term if total is None else total + term
+    projected[...] = total
 
 
-def project(coupling, modes, eigvals):
+def project(coupling, modes):
     rows, depth, columns = coupling.shape[1], coupling.shape[2], modes.shape[2]
-    parts = 4
+    parts = 2
     return pl.pallas_call(
         functools.partial(project_kernel, parts),
-        out_shape=jax.ShapeDtypeStruct((rows, columns), jnp.bfloat16),
-        in_specs=[HBM, HBM, HBM],
+        out_shape=jax.ShapeDtypeStruct((rows, columns), jnp.float32),
+        in_specs=[HBM, HBM],
         out_specs=VMEM,
         scratch_shapes=[
             pltpu.VMEM((rows, depth), jnp.bfloat16),
             pltpu.VMEM((depth, columns), jnp.bfloat16),
-            pltpu.VMEM((1, columns), jnp.float32),
             pltpu.SemaphoreType.DMA((2, parts)),
-            pltpu.SemaphoreType.DMA,
         ],
-        compiler_params=pltpu.CompilerParams(vmem_limit_bytes=53 * 2**20),
+        compiler_params=pltpu.CompilerParams(vmem_limit_bytes=PROJECT_VMEM),
         name="project",
-    )(coupling, modes, eigvals)
+    )(coupling, modes)
 
 
 def update_kernel(other_core, own, sibling, mine, pieces, stiffness, out, made, sems):
@@ -142,14 +139,15 @@
 
 
 def shards(coupling, modes, eigvals, sep_stiffness):
-    scaled = project(coupling, modes, eigvals)
+    projected, eigvals = lax.optimization_barrier((project(coupling, modes), eigvals))
+    scaled = (projected * lax.rsqrt(eigvals[0])[None, :]).astype(jnp.bfloat16)
     bit = lax.axis_index("leaf") % 2
     here = lax.axis_index("panel") // 8 == bit
 
+    sibling = lax.ppermute(scaled, AXES, pairs(to_sibling))
     crossed = lax.ppermute(scaled, AXES, pairs(across))
-    sibling = lax.ppermute(scaled, AXES, pairs(to_sibling))
+    crossed, sibling = lax.optimization_barrier((crossed, sibling))
     held = jnp.where(here, scaled, crossed)
-    held, sibling = lax.optimization_barrier((held, sibling))
     groups = [list(range(core, PANELS, 2)) for core in range(2)]
     sent = jnp.broadcast_to(held[None], (8,) + held.shape)
     mine = lax.all_to_all(sent, "panel", 0, 0, axis_index_groups=groups)

time: 42.4 us -> 41 us (0.967)
  blocking collectives: 14.8 us -> 18.6 us
  starting transfers between devices: 18.9 us -> 15.2 us
  local copies, waits for them, and re-layouts: 0.75 us -> 0.08 us
  waiting for transfers between devices: 2.89 us -> 2.25 us
    ppermute x1, starting transfers between devices: 9.43 us -> 5.48 us  [shards(): sibling = lax.ppermute(scaled, AXES, pairs(to_sibling))]
    all_to_all x1, blocking collectives: 14.8 us -> 18.6 us  [shards(): mine = lax.all_to_all(sent, 'panel', 0, 0, axis_index_groups=groups)]
    unnamed x4, local copies, waits for them, and re-layouts: 0.68 us -> 0.01 us
    ppermute x1, waiting for transfers between devices: 1.86 us -> 1.22 us  [shards(): sibling = lax.ppermute(scaled, AXES, pairs(to_sibling))]
where the time goes in v3:
time: 41 us; the launch traced here: 40.7 us
  blocking collectives  18.6 us (45%)
  starting transfers between devices  15.2 us (37%)
  Pallas kernels  4.44 us (11%)
  waiting for transfers between devices  2.25 us (5%)
    all_to_all x1, blocking collectives, shards(): mine = lax.all_to_all(sent, 'panel', 0, 0, axis_index_groups=groups)  18.6 us
    ppermute x1, starting transfers between devices, shards(): theirs = lax.ppermute(mine, AXES, pairs(to_core))  9 us
    ppermute x1, starting transfers between devices, shards(): sibling = lax.ppermute(scaled, AXES, pairs(to_sibling))  5.48 us
    pallas_call x2, Pallas kernels, update(): pl.pallas_call(kernel, out_shape=jax.ShapeDtypeStruct(stiffness.shape, st...  2.43 us
    pallas_call x1, Pallas kernels, project(): pl.pallas_call(functools.partial(project_kernel, parts), out_shape=jax.Sh...  2 us
    ppermute x1, waiting for transfers between devices, shards(): sibling = lax.ppermute(scaled, AXES, pairs(to_sibling))  1.22 us
    ppermute x1, waiting for transfers between devices, shards(): theirs = lax.ppermute(mine, AXES, pairs(to_core))  1.02 us
  transfers between devices with their start and end apart: 3, of which 2 were waited for; matrix products, arithmetic and copies ran while one was open for 0% of the time, Pallas kernels for 3%

profile of v3, /device:TPU:1, one launch (start us, length us, event | category | flops | bytes accessed | tf_op | source)
XLA Modules:
  0.0 40.7 jit_solution(4297095055243273222)
XLA Ops:
  0.0 0.0 copy-start.1
  0.0 2.0 %project.1 = f32[256,256]{1,0:T(8,128)S(1)} custom-call(bf16[1,256,2048]{2,1,0:T(8,128)(2,1)} %coupling.1, bf16[1,2048,256]{2,1,0:T(8,128)(2,1)} %modes.1), custom_call_target="tpu_custom_call" | custom-call | tf_op jit(solution)/shard_map/project/pallas_call | solution.py:71
  2.0 0.0 copy-done.1
  2.1 5.5 %collective-permute-start.1 = (bf16[256,256]{1,0:T(8,128)(2,1)S(1)}, bf16[256,256]{1,0:T(8,128)(2,1)S(1)}, u32[]{:S(2)}, u32[]{:S(2)}) collective-permute-start(bf16[256,256]{1,0:T(8,128)(2,1)S(1)} %multiply_convert_fusion.own), channel_id=1, source_target_pairs={{0,16},{1,17},{2,18},{3,19},{4,20},{5,21},{6,22},{7,23},{24,8},{25... | collective-permute-start | bytes 393224 | tf_op jit(solution)/shard_map/ppermute | solution.py:147
  7.6 0.7 %collective-permute-start = (bf16[256,256]{1,0:T(8,128)(2,1)S(1)}, bf16[256,256]{1,0:T(8,128)(2,1)S(1)}, u32[]{:S(2)}, u32[]{:S(2)}) collective-permute-start(bf16[256,256]{1,0:T(8,128)(2,1)S(1)} %multiply_convert_fusion.own), channel_id=1, source_target_pairs={{8,22},{9,23},{10,20},{11,21},{12,18},{13,19},{14,16},{15,17},{16,... | collective-permute-start | bytes 393224 | tf_op jit(solution)/shard_map/ppermute | solution.py:148
  8.3 1.2 %collective-permute-done.1.sibling = bf16[256,256]{1,0:T(8,128)(2,1)S(1)} collective-permute-done((bf16[256,256]{1,0:T(8,128)(2,1)S(1)}, bf16[256,256]{1,0:T(8,128)(2,1)S(1)}, u32[]{:S(2)}, u32[]{:S(2)}) %collective-permute-start.1) | collective-permute-done | bytes 131104 | tf_op jit(solution)/shard_map/ppermute | solution.py:147
  9.5 0.0 collective-permute-done
  9.5 0.1 broadcast_in_dim.2
  9.6 0.0 copy-start
  9.6 18.6 %all_to_all.5.mine = bf16[8,256,256]{2,1,0:T(8,128)(2,1)S(1)} all-to-all(bf16[8,256,256]{2,1,0:T(8,128)(2,1)S(1)} %broadcast_in_dim.2), channel_id=1, replica_groups={{0,2,4,6,8,10,12,14},{1,3,5,7,9,11,13,15},{16,18,20,22,24,26,28,30},{17..., dimensions={0} | all-to-all | bytes 2097152 | tf_op jit(solution)/shard_map/all_to_all | solution.py:153
  28.2 9.0 %collective-permute-start.2 = (bf16[8,256,256]{2,1,0:T(8,128)(2,1)S(1)}, bf16[8,256,256]{2,1,0:T(8,128)(2,1)S(1)}, u32[]{:S(2)}, u32[]{:S(2)}) collective-permute-start(bf16[8,256,256]{2,1,0:T(8,128)(2,1)S(1)} %all_to_all.5.mine), channel_id=1, source_target_pairs={{0,1},{1,0},{2,3},{3,2},{4,5},{5,4},{6,7},{7,6},{8,9},{9,8},{10,11... | collective-permute-start | bytes 3145736 | tf_op jit(solution)/shard_map/ppermute | solution.py:154
  37.2 0.0 copy-done
  37.2 1.2 %update_own.1.so_far = bf16[1,256,2048]{2,1,0:T(8,128)(2,1)} custom-call(bf16[256,256]{1,0:T(8,128)(2,1)S(1)} %multiply_convert_fusion.own, bf16[256,256]{1,0:T(8,128)(2,1)S(1)} %collective-permute-done.1.sibling, bf16[8,256,256]{2,1,0:T(8,128)(2,1)S(1)} %all_to_all.5.mine, bf16[1,256,2048]{2,1,0:T(8,128)(2,1)S(1)} %copy-done), custom_call_target="tpu_custom_call" | custom-call | flops 268435456 | bytes 2097152 | tf_op jit(solution)/shard_map/update_own/pallas_call | solution.py:123
  38.4 1.0 %collective-permute-done.2.theirs = bf16[8,256,256]{2,1,0:T(8,128)(2,1)S(1)} collective-permute-done((bf16[8,256,256]{2,1,0:T(8,128)(2,1)S(1)}, bf16[8,256,256]{2,1,0:T(8,128)(2,1)S(1)}, u32[]{:S(2)}, u32[]{:S(2)}) %collective-permute-start.2) | collective-permute-done | bytes 1048608 | tf_op jit(solution)/shard_map/ppermute | solution.py:154
  39.5 1.2 %update_other.1 = bf16[1,256,2048]{2,1,0:T(8,128)(2,1)} custom-call(bf16[256,256]{1,0:T(8,128)(2,1)S(1)} %multiply_convert_fusion.own, bf16[256,256]{1,0:T(8,128)(2,1)S(1)} %collective-permute-done.1.sibling, bf16[8,256,256]{2,1,0:T(8,128)(2,1)S(1)} %all_to_all.5.mine, ...), custom_call_target="tpu_custom_call", output_to_operand_aliasing={{}: (5, {})} | custom-call | flops 268435456 | bytes 2097152 | tf_op jit(solution)/shard_map/update_other/pallas_call | solution.py:123
  (3 shorter events, 0.1 us)
Async XLA Ops:
  0.0 2.0 %copy-start.1 = (f32[1,256]{1,0:T(1,128)S(1)}, f32[1,256]{1,0:T(1,128)}, u32[]{:S(2)}) copy-start(f32[1,256]{1,0:T(1,128)} %param.6) | copy-start | bytes 3076
  2.1 7.4 %collective-permute-start.1 = (bf16[256,256]{1,0:T(8,128)(2,1)S(1)}, bf16[256,256]{1,0:T(8,128)(2,1)S(1)}, u32[]{:S(2)}, u32[]{:S(2)}) collective-permute-start(bf16[256,256]{1,0:T(8,128)(2,1)S(1)} %multiply_convert_fusion.own), channel_id=1, source_target_pairs={{0,16},{1,17},{2,18},{3,19},{4,20},{5,21},{6,22},{7,23},{24,8},{25... | collective-permute-start | bytes 393224 | tf_op jit(solution)/shard_map/ppermute | solution.py:147
  7.6 1.9 %collective-permute-start = (bf16[256,256]{1,0:T(8,128)(2,1)S(1)}, bf16[256,256]{1,0:T(8,128)(2,1)S(1)}, u32[]{:S(2)}, u32[]{:S(2)}) collective-permute-start(bf16[256,256]{1,0:T(8,128)(2,1)S(1)} %multiply_convert_fusion.own), channel_id=1, source_target_pairs={{8,22},{9,23},{10,20},{11,21},{12,18},{13,19},{14,16},{15,17},{16,... | collective-permute-start | bytes 393224 | tf_op jit(solution)/shard_map/ppermute | solution.py:148
  9.6 27.6 %copy-start = (bf16[1,256,2048]{2,1,0:T(8,128)(2,1)S(1)}, bf16[1,256,2048]{2,1,0:T(8,128)(2,1)}, u32[]{:S(2)}) copy-start(bf16[1,256,2048]{2,1,0:T(8,128)(2,1)} %stiffness.3) | copy-start | bytes 3145732
  28.2 11.3 %collective-permute-start.2 = (bf16[8,256,256]{2,1,0:T(8,128)(2,1)S(1)}, bf16[8,256,256]{2,1,0:T(8,128)(2,1)S(1)}, u32[]{:S(2)}, u32[]{:S(2)}) collective-permute-start(bf16[8,256,256]{2,1,0:T(8,128)(2,1)S(1)} %all_to_all.5.mine), channel_id=1, source_target_pairs={{0,1},{1,0},{2,3},{3,2},{4,5},{5,4},{6,7},{7,6},{8,9},{9,8},{10,11... | collective-permute-start | bytes 3145736 | tf_op jit(solution)/shard_map/ppermute | solution.py:154

commit v4 on v3

--- a/solution.py
+++ b/solution.py
@@ -132,7 +132,7 @@
         input_output_aliases={count: 0} if before else {},
         compiler_params=pltpu.CompilerParams(vmem_limit_bytes=16 * 2**20),
         cost_estimate=pl.CostEstimate(
-            flops=2 * rows * 2 * rows * 4 * rows, bytes_accessed=2 * 2**20, transcendentals=0
+            flops=10**8 if before else 10**10, bytes_accessed=2 * 2**20, transcendentals=0
         ),
         name=name,
     )(*arrays, stiffness, *before)
@@ -146,11 +146,15 @@
 
     sibling = lax.ppermute(scaled, AXES, pairs(to_sibling))
     crossed = lax.ppermute(scaled, AXES, pairs(across))
-    crossed, sibling = lax.optimization_barrier((crossed, sibling))
     held = jnp.where(here, scaled, crossed)
     groups = [list(range(core, PANELS, 2)) for core in range(2)]
     sent = jnp.broadcast_to(held[None], (8,) + held.shape)
-    mine = lax.all_to_all(sent, "panel", 0, 0, axis_index_groups=groups)
+    mine = lax.cond(
+        lax.axis_index("panel") < PANELS,
+        lambda x: lax.all_to_all(x, "panel", 0, 0, axis_index_groups=groups),
+        lambda x: x,
+        sent,
+    )
     theirs = lax.ppermute(mine, AXES, pairs(to_core))
     half = update(update_own_kernel, "update_own", (scaled, sibling, mine), sep_stiffness, None)
     return update(update_other_kernel, "update_other", (scaled, sibling, mine, theirs), sep_stiffness, half)

time: 41 us -> 38.9 us (0.949)
  blocking collectives: 18.6 us -> 15.5 us
  starting transfers between devices: 15.2 us -> 17.3 us
  waiting for transfers between devices: 2.25 us -> 1.01 us
    ppermute x1, starting transfers between devices: 5.48 us -> 9.43 us  [shards(): sibling = lax.ppermute(scaled, AXES, pairs(to_sibling))]
    all_to_all x1, blocking collectives: 18.6 us -> 15.5 us  [shards(): lax.all_to_all(x, 'panel', 0, 0, axis_index_groups=groups)]
    ppermute x1, starting transfers between devices: 9 us -> 7.2 us  [shards(): theirs = lax.ppermute(mine, AXES, pairs(to_core))]
    ppermute x1, waiting for transfers between devices: 1.22 us -> 0.01 us  [shards(): sibling = lax.ppermute(scaled, AXES, pairs(to_sibling))]
  transfers between devices with their start and end apart: 3 -> 3, of which waited for: 2 -> 1; matrix products, arithmetic and copies ran while one was open for 0% -> 0% of each run, Pallas kernels for 3% -> 3%
where the time goes in v4:
time: 38.9 us; the launch traced here: 38.7 us
  starting transfers between devices  17.3 us (44%)
  blocking collectives  15.5 us (40%)
  Pallas kernels  4.44 us (11%)
  waiting for transfers between devices  1.01 us (3%)
    all_to_all x1, blocking collectives, shards(): lax.all_to_all(x, 'panel', 0, 0, axis_index_groups=groups)  15.5 us
    ppermute x1, starting transfers between devices, shards(): sibling = lax.ppermute(scaled, AXES, pairs(to_sibling))  9.43 us
    ppermute x1, starting transfers between devices, shards(): theirs = lax.ppermute(mine, AXES, pairs(to_core))  7.2 us
    pallas_call x2, Pallas kernels, update(): pl.pallas_call(kernel, out_shape=jax.ShapeDtypeStruct(stiffness.shape, st...  2.44 us
    pallas_call x1, Pallas kernels, project(): pl.pallas_call(functools.partial(project_kernel, parts), out_shape=jax.Sh...  2 us
    ppermute x1, waiting for transfers between devices, shards(): theirs = lax.ppermute(mine, AXES, pairs(to_core))  1.01 us
  transfers between devices with their start and end apart: 3, of which 1 were waited for; matrix products, arithmetic and copies ran while one was open for 0% of the time, Pallas kernels for 3%

profile of v4, /device:TPU:1, one launch (start us, length us, event | category | flops | bytes accessed | tf_op | source)
XLA Modules:
  0.0 38.7 jit_solution(14008275599952199520)
XLA Ops:
  0.0 0.0 copy-start.1
  0.0 2.0 %project.1 = f32[256,256]{1,0:T(8,128)S(1)} custom-call(bf16[1,256,2048]{2,1,0:T(8,128)(2,1)} %coupling.1, bf16[1,2048,256]{2,1,0:T(8,128)(2,1)} %modes.1), custom_call_target="tpu_custom_call" | custom-call | tf_op jit(solution)/shard_map/project/pallas_call | solution.py:71
  2.0 0.0 copy-done.1
  2.1 0.7 %collective-permute-start.1 = (bf16[256,256]{1,0:T(8,128)(2,1)S(1)}, bf16[256,256]{1,0:T(8,128)(2,1)S(1)}, u32[]{:S(2)}, u32[]{:S(2)}) collective-permute-start(bf16[256,256]{1,0:T(8,128)(2,1)S(1)} %multiply_convert_fusion.own), channel_id=1, source_target_pairs={{8,22},{9,23},{10,20},{11,21},{12,18},{13,19},{14,16},{15,17},{16,... | collective-permute-start | bytes 393224 | tf_op jit(solution)/shard_map/ppermute | solution.py:148
  2.7 9.4 %collective-permute-start = (bf16[256,256]{1,0:T(8,128)(2,1)S(1)}, bf16[256,256]{1,0:T(8,128)(2,1)S(1)}, u32[]{:S(2)}, u32[]{:S(2)}) collective-permute-start(bf16[256,256]{1,0:T(8,128)(2,1)S(1)} %multiply_convert_fusion.own), channel_id=1, source_target_pairs={{0,16},{1,17},{2,18},{3,19},{4,20},{5,21},{6,22},{7,23},{24,8},{25... | collective-permute-start | bytes 393224 | tf_op jit(solution)/shard_map/ppermute | solution.py:147
  12.2 0.0 collective-permute-done.1
  12.3 0.1 broadcast_in_dim.7
  12.3 0.0 copy-start
  12.3 15.6 %conditional.1 = (bf16[8,256,256]{2,1,0:T(8,128)(2,1)S(1)}) conditional(s32[]{:T(128)} %convert_element_type.7, bf16[8,256,256]{2,1,0:T(8,128)(2,1)S(1)} %broadcast_in_dim.7, bf16[8,256,256]{2,1,0:T(8,128)(2,1)S(1)} %broadcast_in_dim.7), branch_computations={%region_0.1_spmd, %region_1.2_spmd} | conditional | bytes 4194312 | solution.py:152
  12.4 0.1 copy.9
  12.4 15.5 %all_to_all.4 = bf16[8,256,256]{2,1,0:T(8,128)(2,1)S(1)} all-to-all(bf16[8,256,256]{2,1,0:T(8,128)(2,1)S(1)} %copy.9), channel_id=1, replica_groups={{0,2,4,6,8,10,12,14},{1,3,5,7,9,11,13,15},{16,18,20,22,24,26,28,30},{17..., dimensions={0} | all-to-all | bytes 2097152 | tf_op jit(solution)/shard_map/cond/branch_1_fun/all_to_all | solution.py:154
  28.0 7.2 %collective-permute-start.2 = (bf16[8,256,256]{2,1,0:T(8,128)(2,1)S(1)}, bf16[8,256,256]{2,1,0:T(8,128)(2,1)S(1)}, u32[]{:S(2)}, u32[]{:S(2)}) collective-permute-start(bf16[8,256,256]{2,1,0:T(8,128)(2,1)S(1)} %get-tuple-element.14.mine), channel_id=1, source_target_pairs={{0,1},{1,0},{2,3},{3,2},{4,5},{5,4},{6,7},{7,6},{8,9},{9,8},{10,11... | collective-permute-start | bytes 3145736 | tf_op jit(solution)/shard_map/ppermute | solution.py:158
  35.2 0.0 collective-permute-done.sibling
  35.2 0.0 copy-done
  35.2 1.2 %update_own.1.so_far = bf16[1,256,2048]{2,1,0:T(8,128)(2,1)} custom-call(bf16[256,256]{1,0:T(8,128)(2,1)S(1)} %multiply_convert_fusion.own, bf16[256,256]{1,0:T(8,128)(2,1)S(1)} %collective-permute-done.sibling, bf16[8,256,256]{2,1,0:T(8,128)(2,1)S(1)} %get-tuple-element.14.mine, bf16[1,256,2048]{2,1,0:T(8,128)(2,1)S(1)} %copy-done), custom_call_target="tpu_custom_call" | custom-call | flops 10000000000 | bytes 2097152 | tf_op jit(solution)/shard_map/update_own/pallas_call | solution.py:123
  36.4 1.0 %collective-permute-done.2.theirs = bf16[8,256,256]{2,1,0:T(8,128)(2,1)S(1)} collective-permute-done((bf16[8,256,256]{2,1,0:T(8,128)(2,1)S(1)}, bf16[8,256,256]{2,1,0:T(8,128)(2,1)S(1)}, u32[]{:S(2)}, u32[]{:S(2)}) %collective-permute-start.2) | collective-permute-done | bytes 1048608 | tf_op jit(solution)/shard_map/ppermute | solution.py:158
  37.5 1.2 %update_other.1 = bf16[1,256,2048]{2,1,0:T(8,128)(2,1)} custom-call(bf16[256,256]{1,0:T(8,128)(2,1)S(1)} %multiply_convert_fusion.own, bf16[256,256]{1,0:T(8,128)(2,1)S(1)} %collective-permute-done.sibling, bf16[8,256,256]{2,1,0:T(8,128)(2,1)S(1)} %get-tuple-element.14.mine, ...), custom_call_target="tpu_custom_call", output_to_operand_aliasing={{}: (5, {})} | custom-call | flops 100000000 | bytes 2097152 | tf_op jit(solution)/shard_map/update_other/pallas_call | solution.py:123
  (3 shorter events, 0.1 us)
Async XLA Ops:
  0.0 2.0 %copy-start.1 = (f32[1,256]{1,0:T(1,128)S(1)}, f32[1,256]{1,0:T(1,128)}, u32[]{:S(2)}) copy-start(f32[1,256]{1,0:T(1,128)} %param.8) | copy-start | bytes 3076
  2.1 10.1 %collective-permute-start.1 = (bf16[256,256]{1,0:T(8,128)(2,1)S(1)}, bf16[256,256]{1,0:T(8,128)(2,1)S(1)}, u32[]{:S(2)}, u32[]{:S(2)}) collective-permute-start(bf16[256,256]{1,0:T(8,128)(2,1)S(1)} %multiply_convert_fusion.own), channel_id=1, source_target_pairs={{8,22},{9,23},{10,20},{11,21},{12,18},{13,19},{14,16},{15,17},{16,... | collective-permute-start | bytes 393224 | tf_op jit(solution)/shard_map/ppermute | solution.py:148
  2.7 32.4 %collective-permute-start = (bf16[256,256]{1,0:T(8,128)(2,1)S(1)}, bf16[256,256]{1,0:T(8,128)(2,1)S(1)}, u32[]{:S(2)}, u32[]{:S(2)}) collective-permute-start(bf16[256,256]{1,0:T(8,128)(2,1)S(1)} %multiply_convert_fusion.own), channel_id=1, source_target_pairs={{0,16},{1,17},{2,18},{3,19},{4,20},{5,21},{6,22},{7,23},{24,8},{25... | collective-permute-start | bytes 393224 | tf_op jit(solution)/shard_map/ppermute | solution.py:147
  12.3 22.9 %copy-start = (bf16[1,256,2048]{2,1,0:T(8,128)(2,1)S(1)}, bf16[1,256,2048]{2,1,0:T(8,128)(2,1)}, u32[]{:S(2)}) copy-start(bf16[1,256,2048]{2,1,0:T(8,128)(2,1)} %stiffness.3) | copy-start | bytes 3145732
  28.0 9.5 %collective-permute-start.2 = (bf16[8,256,256]{2,1,0:T(8,128)(2,1)S(1)}, bf16[8,256,256]{2,1,0:T(8,128)(2,1)S(1)}, u32[]{:S(2)}, u32[]{:S(2)}) collective-permute-start(bf16[8,256,256]{2,1,0:T(8,128)(2,1)S(1)} %get-tuple-element.14.mine), channel_id=1, source_target_pairs={{0,1},{1,0},{2,3},{3,2},{4,5},{5,4},{6,7},{7,6},{8,9},{9,8},{10,11... | collective-permute-start | bytes 3145736 | tf_op jit(solution)/shard_map/ppermute | solution.py:158

commit v5 on v4

--- a/solution.py
+++ b/solution.py
@@ -28,8 +28,20 @@
     return found
 
 
-def across(bit, panel):
-    return None if panel // 8 == bit else (1 - bit, panel ^ 14)
+def shift(bit, panel):
+    if panel // 8 == bit:
+        return (bit, panel ^ 12) if (bit, panel) != (0, 0) else None
+    return (1 - bit, panel ^ 2) if (bit, panel) != (1, 2) else (0, 12)
+
+
+def own_at(bit, core, n):
+    usual = (1 - bit) * 4 + (n ^ 2)
+    return jnp.where((bit == 0) & (core == 0), 0, usual) if n == 0 else usual
+
+
+def other_at(bit, core, n):
+    usual = bit * 4 + (n ^ 1)
+    return jnp.where((bit == 0) & (core == 0) & (n == 1), 6, usual)
 
 
 def to_sibling(bit, panel):
@@ -88,15 +100,17 @@
     core = 1 - panel % 2 if other_core else panel % 2
     here = panel // 8 == bit
     width = own.shape[0]
-    partner = jnp.where(here, mine[(1 - bit) * 4 + 3 - (panel % 8) // 2], sibling[...])
+    place = panel % 8 // 2
+    partner = mine[other_at(bit, panel % 2, place)]
+    partner = jnp.where(here, partner, sibling[...])
     stores = []
     for n in range(4):
         cut = pl.ds(pl.multiple_of((2 * n + core) * width, width), width)
         block = lax.dot_general(
-            own[...], pieces[bit * 4 + n], (((1,), (1,)), ((), ())), preferred_element_type=jnp.float32
+            own[...], pieces[own_at(bit, core, n)], (((1,), (1,)), ((), ())), preferred_element_type=jnp.float32
         ) + lax.dot_general(
             partner,
-            pieces[(1 - bit) * 4 + 3 - n],
+            pieces[other_at(bit, core, n)],
             (((1,), (1,)), ((), ())),
             preferred_element_type=jnp.float32,
         )
@@ -138,22 +152,24 @@
     )(*arrays, stiffness, *before)
 
 
+def spread(piece):
+    return jnp.broadcast_to(piece[None], (8,) + piece.shape)
+
+
 def shards(coupling, modes, eigvals, sep_stiffness):
     projected, eigvals = lax.optimization_barrier((project(coupling, modes), eigvals))
     scaled = (projected * lax.rsqrt(eigvals[0])[None, :]).astype(jnp.bfloat16)
-    bit = lax.axis_index("leaf") % 2
-    here = lax.axis_index("panel") // 8 == bit
-
+    bit, panel = lax.axis_index("leaf") % 2, lax.axis_index("panel")
     sibling = lax.ppermute(scaled, AXES, pairs(to_sibling))
-    crossed = lax.ppermute(scaled, AXES, pairs(across))
-    held = jnp.where(here, scaled, crossed)
+    moved = lax.ppermute(scaled, AXES, pairs(shift))
+    keeps = (bit == 0) & (panel == 0)
+    held = jnp.where(keeps, scaled, moved)
     groups = [list(range(core, PANELS, 2)) for core in range(2)]
-    sent = jnp.broadcast_to(held[None], (8,) + held.shape)
     mine = lax.cond(
         lax.axis_index("panel") < PANELS,
-        lambda x: lax.all_to_all(x, "panel", 0, 0, axis_index_groups=groups),
-        lambda x: x,
-        sent,
+        lambda x: lax.all_to_all(spread(x), "panel", 0, 0, axis_index_groups=groups),
+        spread,
+        held,
     )
     theirs = lax.ppermute(mine, AXES, pairs(to_core))
     half = update(update_own_kernel, "update_own", (scaled, sibling, mine), sep_stiffness, None)

time: 38.9 us -> 38 us (0.977)
  starting transfers between devices: 17.3 us -> 16.2 us
  blocking collectives: 15.5 us -> 15.9 us
    ppermute x1, starting transfers between devices: 9.43 us -> 2.18 us  [shards(): sibling = lax.ppermute(scaled, AXES, pairs(to_sibling))]
    ppermute x1, starting transfers between devices: 0.67 us -> 5.47 us  [shards(): moved = lax.ppermute(scaled, AXES, pairs(shift))]
    ppermute x1, starting transfers between devices: 7.2 us -> 8.57 us  [shards(): theirs = lax.ppermute(mine, AXES, pairs(to_core))]
where the time goes in v5:
time: 38 us; the launch traced here: 37.8 us
  starting transfers between devices  16.2 us (43%)
  blocking collectives  15.9 us (42%)
  Pallas kernels  4.43 us (12%)
  waiting for transfers between devices  1.02 us (3%)
    all_to_all x1, blocking collectives, shards(): lax.all_to_all(spread(x), 'panel', 0, 0, axis_index_groups=groups)  15.9 us
    ppermute x1, starting transfers between devices, shards(): theirs = lax.ppermute(mine, AXES, pairs(to_core))  8.57 us
    ppermute x1, starting transfers between devices, shards(): moved = lax.ppermute(scaled, AXES, pairs(shift))  5.47 us
    pallas_call x2, Pallas kernels, update(): pl.pallas_call(kernel, out_shape=jax.ShapeDtypeStruct(stiffness.shape, st...  2.43 us
    ppermute x1, starting transfers between devices, shards(): sibling = lax.ppermute(scaled, AXES, pairs(to_sibling))  2.18 us
    pallas_call x1, Pallas kernels, project(): pl.pallas_call(functools.partial(project_kernel, parts), out_shape=jax.Sh...  2 us
    ppermute x1, waiting for transfers between devices, shards(): theirs = lax.ppermute(mine, AXES, pairs(to_core))  1.01 us
  transfers between devices with their start and end apart: 3, of which 1 were waited for; matrix products, arithmetic and copies ran while one was open for 0% of the time, Pallas kernels for 3%

profile of v5, /device:TPU:1, one launch (start us, length us, event | category | flops | bytes accessed | tf_op | source)
XLA Modules:
  0.0 37.8 jit_solution(2894428421809976706)
XLA Ops:
  0.0 0.0 copy-start.1
  0.0 2.0 %project.1 = f32[256,256]{1,0:T(8,128)S(1)} custom-call(bf16[1,256,2048]{2,1,0:T(8,128)(2,1)} %coupling.1, bf16[1,2048,256]{2,1,0:T(8,128)(2,1)} %modes.1), custom_call_target="tpu_custom_call" | custom-call | tf_op jit(solution)/shard_map/project/pallas_call | solution.py:83
  2.0 0.0 copy-done.1
  2.1 5.5 %collective-permute-start.1 = (bf16[256,256]{1,0:T(8,128)(2,1)S(1)}, bf16[256,256]{1,0:T(8,128)(2,1)S(1)}, u32[]{:S(2)}, u32[]{:S(2)}) collective-permute-start(bf16[256,256]{1,0:T(8,128)(2,1)S(1)} %multiply_convert_fusion.own), channel_id=1, source_target_pairs={{1,13},{2,14},{3,15},{4,8},{5,9},{6,10},{7,11},{8,26},{9,27},{10,2... | collective-permute-start | bytes 393224 | tf_op jit(solution)/shard_map/ppermute | solution.py:164
  7.5 2.2 %collective-permute-start = (bf16[256,256]{1,0:T(8,128)(2,1)S(1)}, bf16[256,256]{1,0:T(8,128)(2,1)S(1)}, u32[]{:S(2)}, u32[]{:S(2)}) collective-permute-start(bf16[256,256]{1,0:T(8,128)(2,1)S(1)} %multiply_convert_fusion.own), channel_id=1, source_target_pairs={{0,16},{1,17},{2,18},{3,19},{4,20},{5,21},{6,22},{7,23},{24,8},{25... | collective-permute-start | bytes 393224 | tf_op jit(solution)/shard_map/ppermute | solution.py:163
  9.7 0.0 collective-permute-done.1
  9.8 0.0 copy-start
  9.8 15.9 %conditional.1 = (bf16[8,256,256]{2,1,0:T(8,128)(2,1)S(1)}) conditional(s32[]{:T(128)} %convert_element_type.7, bf16[256,256]{1,0:T(8,128)(2,1)S(1)} %broadcast_select_fusion, bf16[256,256]{1,0:T(8,128)(2,1)S(1)} %broadcast_select_fusion), branch_computations={%region_0.1_spmd, %region_1.2_spmd} | conditional | bytes 3276808 | solution.py:168
  9.8 0.1 broadcast_in_dim.2
  9.9 15.9 %all_to_all.4 = bf16[8,256,256]{2,1,0:T(8,128)(2,1)S(1)} all-to-all(bf16[8,256,256]{2,1,0:T(8,128)(2,1)S(1)} %broadcast_in_dim.2), channel_id=1, replica_groups={{0,2,4,6,8,10,12,14},{1,3,5,7,9,11,13,15},{16,18,20,22,24,26,28,30},{17..., dimensions={0} | all-to-all | bytes 2097152 | tf_op jit(solution)/shard_map/cond/branch_1_fun/all_to_all | solution.py:170
  25.7 8.6 %collective-permute-start.2 = (bf16[8,256,256]{2,1,0:T(8,128)(2,1)S(1)}, bf16[8,256,256]{2,1,0:T(8,128)(2,1)S(1)}, u32[]{:S(2)}, u32[]{:S(2)}) collective-permute-start(bf16[8,256,256]{2,1,0:T(8,128)(2,1)S(1)} %get-tuple-element.14.mine), channel_id=1, source_target_pairs={{0,1},{1,0},{2,3},{3,2},{4,5},{5,4},{6,7},{7,6},{8,9},{9,8},{10,11... | collective-permute-start | bytes 3145736 | tf_op jit(solution)/shard_map/ppermute | solution.py:174
  34.3 0.0 collective-permute-done.sibling
  34.3 0.0 copy-done
  34.3 1.2 %update_own.1.so_far = bf16[1,256,2048]{2,1,0:T(8,128)(2,1)} custom-call(bf16[256,256]{1,0:T(8,128)(2,1)S(1)} %multiply_convert_fusion.own, bf16[256,256]{1,0:T(8,128)(2,1)S(1)} %collective-permute-done.sibling, bf16[8,256,256]{2,1,0:T(8,128)(2,1)S(1)} %get-tuple-element.14.mine, bf16[1,256,2048]{2,1,0:T(8,128)(2,1)S(1)} %copy-done), custom_call_target="tpu_custom_call" | custom-call | flops 10000000000 | bytes 2097152 | tf_op jit(solution)/shard_map/update_own/pallas_call | solution.py:137
  35.6 1.0 %collective-permute-done.2.theirs = bf16[8,256,256]{2,1,0:T(8,128)(2,1)S(1)} collective-permute-done((bf16[8,256,256]{2,1,0:T(8,128)(2,1)S(1)}, bf16[8,256,256]{2,1,0:T(8,128)(2,1)S(1)}, u32[]{:S(2)}, u32[]{:S(2)}) %collective-permute-start.2) | collective-permute-done | bytes 1048608 | tf_op jit(solution)/shard_map/ppermute | solution.py:174
  36.6 1.2 %update_other.1 = bf16[1,256,2048]{2,1,0:T(8,128)(2,1)} custom-call(bf16[256,256]{1,0:T(8,128)(2,1)S(1)} %multiply_convert_fusion.own, bf16[256,256]{1,0:T(8,128)(2,1)S(1)} %collective-permute-done.sibling, bf16[8,256,256]{2,1,0:T(8,128)(2,1)S(1)} %get-tuple-element.14.mine, ...), custom_call_target="tpu_custom_call", output_to_operand_aliasing={{}: (5, {})} | custom-call | flops 100000000 | bytes 2097152 | tf_op jit(solution)/shard_map/update_other/pallas_call | solution.py:137
  (3 shorter events, 0.1 us)
Async XLA Ops:
  0.0 2.0 %copy-start.1 = (f32[1,256]{1,0:T(1,128)S(1)}, f32[1,256]{1,0:T(1,128)}, u32[]{:S(2)}) copy-start(f32[1,256]{1,0:T(1,128)} %param.8) | copy-start | bytes 3076
  2.1 7.7 %collective-permute-start.1 = (bf16[256,256]{1,0:T(8,128)(2,1)S(1)}, bf16[256,256]{1,0:T(8,128)(2,1)S(1)}, u32[]{:S(2)}, u32[]{:S(2)}) collective-permute-start(bf16[256,256]{1,0:T(8,128)(2,1)S(1)} %multiply_convert_fusion.own), channel_id=1, source_target_pairs={{1,13},{2,14},{3,15},{4,8},{5,9},{6,10},{7,11},{8,26},{9,27},{10,2... | collective-permute-start | bytes 393224 | tf_op jit(solution)/shard_map/ppermute | solution.py:164
  7.5 26.8 %collective-permute-start = (bf16[256,256]{1,0:T(8,128)(2,1)S(1)}, bf16[256,256]{1,0:T(8,128)(2,1)S(1)}, u32[]{:S(2)}, u32[]{:S(2)}) collective-permute-start(bf16[256,256]{1,0:T(8,128)(2,1)S(1)} %multiply_convert_fusion.own), channel_id=1, source_target_pairs={{0,16},{1,17},{2,18},{3,19},{4,20},{5,21},{6,22},{7,23},{24,8},{25... | collective-permute-start | bytes 393224 | tf_op jit(solution)/shard_map/ppermute | solution.py:163
  9.8 24.5 %copy-start = (bf16[1,256,2048]{2,1,0:T(8,128)(2,1)S(1)}, bf16[1,256,2048]{2,1,0:T(8,128)(2,1)}, u32[]{:S(2)}) copy-start(bf16[1,256,2048]{2,1,0:T(8,128)(2,1)} %stiffness.3) | copy-start | bytes 3145732
  25.7 10.8 %collective-permute-start.2 = (bf16[8,256,256]{2,1,0:T(8,128)(2,1)S(1)}, bf16[8,256,256]{2,1,0:T(8,128)(2,1)S(1)}, u32[]{:S(2)}, u32[]{:S(2)}) collective-permute-start(bf16[8,256,256]{2,1,0:T(8,128)(2,1)S(1)} %get-tuple-element.14.mine), channel_id=1, source_target_pairs={{0,1},{1,0},{2,3},{3,2},{4,5},{5,4},{6,7},{7,6},{8,9},{9,8},{10,11... | collective-permute-start | bytes 3145736 | tf_op jit(solution)/shard_map/ppermute | solution.py:174

commit v6 on v5

--- a/solution.py
+++ b/solution.py
@@ -19,7 +19,7 @@
     for parent in range(lax.axis_size("leaf") // 2):
         for bit in range(2):
             for panel in range(PANELS):
-                target = move(bit, panel)
+                target = move(parent, bit, panel)
                 if target is not None:
                     found.append((
                         (2 * parent + bit) * PANELS + panel,
@@ -28,27 +28,27 @@
     return found
 
 
-def shift(bit, panel):
+def shift(parent, bit, panel):
     if panel // 8 == bit:
-        return (bit, panel ^ 12) if (bit, panel) != (0, 0) else None
-    return (1 - bit, panel ^ 2) if (bit, panel) != (1, 2) else (0, 12)
+        return (bit, panel ^ 12) if (parent, bit, panel) != (0, 0, 0) else None
+    return (1 - bit, panel ^ 2) if (parent, bit, panel) != (0, 1, 2) else (0, 12)
 
 
-def own_at(bit, core, n):
-    usual = (1 - bit) * 4 + (n ^ 2)
-    return jnp.where((bit == 0) & (core == 0), 0, usual) if n == 0 else usual
+def own_at(leaf, core, n):
+    usual = (1 - leaf % 2) * 4 + (n ^ 2)
+    return jnp.where((leaf == 0) & (core == 0), 0, usual) if n == 0 else usual
 
 
-def other_at(bit, core, n):
-    usual = bit * 4 + (n ^ 1)
-    return jnp.where((bit == 0) & (core == 0) & (n == 1), 6, usual)
+def other_at(leaf, core, n):
+    usual = leaf % 2 * 4 + (n ^ 1)
+    return jnp.where((leaf == 0) & (core == 0) & (n == 1), 6, usual)
 
 
-def to_sibling(bit, panel):
+def to_sibling(parent, bit, panel):
     return (1 - bit, panel) if panel // 8 == bit else None
 
 
-def to_core(bit, panel):
+def to_core(parent, bit, panel):
     return (bit, panel ^ 1)
 
 
@@ -96,21 +96,21 @@
 
 
 def update_kernel(other_core, own, sibling, mine, pieces, stiffness, out, made, sems):
-    bit, panel = lax.axis_index("leaf") % 2, lax.axis_index("panel")
+    leaf, panel = lax.axis_index("leaf"), lax.axis_index("panel")
     core = 1 - panel % 2 if other_core else panel % 2
-    here = panel // 8 == bit
+    here = panel // 8 == leaf % 2
     width = own.shape[0]
     place = panel % 8 // 2
-    partner = mine[other_at(bit, panel % 2, place)]
+    partner = mine[other_at(leaf, panel % 2, place)]
     partner = jnp.where(here, partner, sibling[...])
     stores = []
     for n in range(4):
         cut = pl.ds(pl.multiple_of((2 * n + core) * width, width), width)
         block = lax.dot_general(
-            own[...], pieces[own_at(bit, core, n)], (((1,), (1,)), ((), ())), preferred_element_type=jnp.float32
+            own[...], pieces[own_at(leaf, core, n)], (((1,), (1,)), ((), ())), preferred_element_type=jnp.float32
         ) + lax.dot_general(
             partner,
-            pieces[other_at(bit, core, n)],
+            pieces[other_at(leaf, core, n)],
             (((1,), (1,)), ((), ())),
             preferred_element_type=jnp.float32,
         )
@@ -159,10 +159,10 @@
 def shards(coupling, modes, eigvals, sep_stiffness):
     projected, eigvals = lax.optimization_barrier((project(coupling, modes), eigvals))
     scaled = (projected * lax.rsqrt(eigvals[0])[None, :]).astype(jnp.bfloat16)
-    bit, panel = lax.axis_index("leaf") % 2, lax.axis_index("panel")
+    leaf, panel = lax.axis_index("leaf"), lax.axis_index("panel")
     sibling = lax.ppermute(scaled, AXES, pairs(to_sibling))
     moved = lax.ppermute(scaled, AXES, pairs(shift))
-    keeps = (bit == 0) & (panel == 0)
+    keeps = (leaf == 0) & (panel == 0)
     held = jnp.where(keeps, scaled, moved)
     groups = [list(range(core, PANELS, 2)) for core in range(2)]
     mine = lax.cond(

time: 38 us -> 38 us (level)
  no operation moved by 1% of the time
where the time goes in v6:
time: 38 us; the launch traced here: 37.8 us
  starting transfers between devices  16.2 us (43%)
  blocking collectives  15.9 us (42%)
  Pallas kernels  4.43 us (12%)
  waiting for transfers between devices  1.02 us (3%)
    all_to_all x1, blocking collectives, shards(): lax.all_to_all(spread(x), 'panel', 0, 0, axis_index_groups=groups)  15.9 us
    ppermute x1, starting transfers between devices, shards(): theirs = lax.ppermute(mine, AXES, pairs(to_core))  8.57 us
    ppermute x1, starting transfers between devices, shards(): moved = lax.ppermute(scaled, AXES, pairs(shift))  5.47 us
    pallas_call x2, Pallas kernels, update(): pl.pallas_call(kernel, out_shape=jax.ShapeDtypeStruct(stiffness.shape, st...  2.43 us
    ppermute x1, starting transfers between devices, shards(): sibling = lax.ppermute(scaled, AXES, pairs(to_sibling))  2.18 us
    pallas_call x1, Pallas kernels, project(): pl.pallas_call(functools.partial(project_kernel, parts), out_shape=jax.Sh...  2 us
    ppermute x1, waiting for transfers between devices, shards(): theirs = lax.ppermute(mine, AXES, pairs(to_core))  1.01 us
  transfers between devices with their start and end apart: 3, of which 1 were waited for; matrix products, arithmetic and copies ran while one was open for 0% of the time, Pallas kernels for 3%

profile of v6, /device:TPU:1, one launch (start us, length us, event | category | flops | bytes accessed | tf_op | source)
XLA Modules:
  0.0 37.8 jit_solution(9640699130830498240)
XLA Ops:
  0.0 0.0 copy-start.1
  0.0 2.0 %project.1 = f32[256,256]{1,0:T(8,128)S(1)} custom-call(bf16[1,256,2048]{2,1,0:T(8,128)(2,1)} %coupling.1, bf16[1,2048,256]{2,1,0:T(8,128)(2,1)} %modes.1), custom_call_target="tpu_custom_call" | custom-call | tf_op jit(solution)/shard_map/project/pallas_call | solution.py:83
  2.0 0.0 copy-done.1
  2.1 5.5 %collective-permute-start.1 = (bf16[256,256]{1,0:T(8,128)(2,1)S(1)}, bf16[256,256]{1,0:T(8,128)(2,1)S(1)}, u32[]{:S(2)}, u32[]{:S(2)}) collective-permute-start(bf16[256,256]{1,0:T(8,128)(2,1)S(1)} %multiply_convert_fusion.own), channel_id=1, source_target_pairs={{1,13},{2,14},{3,15},{4,8},{5,9},{6,10},{7,11},{8,26},{9,27},{10,2... | collective-permute-start | bytes 393224 | tf_op jit(solution)/shard_map/ppermute | solution.py:164
  7.5 2.2 %collective-permute-start = (bf16[256,256]{1,0:T(8,128)(2,1)S(1)}, bf16[256,256]{1,0:T(8,128)(2,1)S(1)}, u32[]{:S(2)}, u32[]{:S(2)}) collective-permute-start(bf16[256,256]{1,0:T(8,128)(2,1)S(1)} %multiply_convert_fusion.own), channel_id=1, source_target_pairs={{0,16},{1,17},{2,18},{3,19},{4,20},{5,21},{6,22},{7,23},{24,8},{25... | collective-permute-start | bytes 393224 | tf_op jit(solution)/shard_map/ppermute | solution.py:163
  9.7 0.0 collective-permute-done.1
  9.8 0.0 copy-start
  9.8 15.9 %conditional.1 = (bf16[8,256,256]{2,1,0:T(8,128)(2,1)S(1)}) conditional(s32[]{:T(128)} %convert_element_type.7, bf16[256,256]{1,0:T(8,128)(2,1)S(1)} %broadcast_select_fusion, bf16[256,256]{1,0:T(8,128)(2,1)S(1)} %broadcast_select_fusion), branch_computations={%region_0.1_spmd, %region_1.2_spmd} | conditional | bytes 3276808 | solution.py:168
  9.8 0.1 broadcast_in_dim.2
  9.9 15.9 %all_to_all.4 = bf16[8,256,256]{2,1,0:T(8,128)(2,1)S(1)} all-to-all(bf16[8,256,256]{2,1,0:T(8,128)(2,1)S(1)} %broadcast_in_dim.2), channel_id=1, replica_groups={{0,2,4,6,8,10,12,14},{1,3,5,7,9,11,13,15},{16,18,20,22,24,26,28,30},{17..., dimensions={0} | all-to-all | bytes 2097152 | tf_op jit(solution)/shard_map/cond/branch_1_fun/all_to_all | solution.py:170
  25.7 8.6 %collective-permute-start.2 = (bf16[8,256,256]{2,1,0:T(8,128)(2,1)S(1)}, bf16[8,256,256]{2,1,0:T(8,128)(2,1)S(1)}, u32[]{:S(2)}, u32[]{:S(2)}) collective-permute-start(bf16[8,256,256]{2,1,0:T(8,128)(2,1)S(1)} %get-tuple-element.14.mine), channel_id=1, source_target_pairs={{0,1},{1,0},{2,3},{3,2},{4,5},{5,4},{6,7},{7,6},{8,9},{9,8},{10,11... | collective-permute-start | bytes 3145736 | tf_op jit(solution)/shard_map/ppermute | solution.py:174
  34.3 0.0 collective-permute-done.sibling
  34.3 0.0 copy-done
  34.3 1.2 %update_own.1.so_far = bf16[1,256,2048]{2,1,0:T(8,128)(2,1)} custom-call(bf16[256,256]{1,0:T(8,128)(2,1)S(1)} %multiply_convert_fusion.own, bf16[256,256]{1,0:T(8,128)(2,1)S(1)} %collective-permute-done.sibling, bf16[8,256,256]{2,1,0:T(8,128)(2,1)S(1)} %get-tuple-element.14.mine, bf16[1,256,2048]{2,1,0:T(8,128)(2,1)S(1)} %copy-done), custom_call_target="tpu_custom_call" | custom-call | flops 10000000000 | bytes 2097152 | tf_op jit(solution)/shard_map/update_own/pallas_call | solution.py:137
  35.6 1.0 %collective-permute-done.2.theirs = bf16[8,256,256]{2,1,0:T(8,128)(2,1)S(1)} collective-permute-done((bf16[8,256,256]{2,1,0:T(8,128)(2,1)S(1)}, bf16[8,256,256]{2,1,0:T(8,128)(2,1)S(1)}, u32[]{:S(2)}, u32[]{:S(2)}) %collective-permute-start.2) | collective-permute-done | bytes 1048608 | tf_op jit(solution)/shard_map/ppermute | solution.py:174
  36.6 1.2 %update_other.1 = bf16[1,256,2048]{2,1,0:T(8,128)(2,1)} custom-call(bf16[256,256]{1,0:T(8,128)(2,1)S(1)} %multiply_convert_fusion.own, bf16[256,256]{1,0:T(8,128)(2,1)S(1)} %collective-permute-done.sibling, bf16[8,256,256]{2,1,0:T(8,128)(2,1)S(1)} %get-tuple-element.14.mine, ...), custom_call_target="tpu_custom_call", output_to_operand_aliasing={{}: (5, {})} | custom-call | flops 100000000 | bytes 2097152 | tf_op jit(solution)/shard_map/update_other/pallas_call | solution.py:137
  (3 shorter events, 0.1 us)
Async XLA Ops:
  0.0 2.0 %copy-start.1 = (f32[1,256]{1,0:T(1,128)S(1)}, f32[1,256]{1,0:T(1,128)}, u32[]{:S(2)}) copy-start(f32[1,256]{1,0:T(1,128)} %param.8) | copy-start | bytes 3076
  2.1 7.7 %collective-permute-start.1 = (bf16[256,256]{1,0:T(8,128)(2,1)S(1)}, bf16[256,256]{1,0:T(8,128)(2,1)S(1)}, u32[]{:S(2)}, u32[]{:S(2)}) collective-permute-start(bf16[256,256]{1,0:T(8,128)(2,1)S(1)} %multiply_convert_fusion.own), channel_id=1, source_target_pairs={{1,13},{2,14},{3,15},{4,8},{5,9},{6,10},{7,11},{8,26},{9,27},{10,2... | collective-permute-start | bytes 393224 | tf_op jit(solution)/shard_map/ppermute | solution.py:164
  7.5 26.8 %collective-permute-start = (bf16[256,256]{1,0:T(8,128)(2,1)S(1)}, bf16[256,256]{1,0:T(8,128)(2,1)S(1)}, u32[]{:S(2)}, u32[]{:S(2)}) collective-permute-start(bf16[256,256]{1,0:T(8,128)(2,1)S(1)} %multiply_convert_fusion.own), channel_id=1, source_target_pairs={{0,16},{1,17},{2,18},{3,19},{4,20},{5,21},{6,22},{7,23},{24,8},{25... | collective-permute-start | bytes 393224 | tf_op jit(solution)/shard_map/ppermute | solution.py:163
  9.8 24.5 %copy-start = (bf16[1,256,2048]{2,1,0:T(8,128)(2,1)S(1)}, bf16[1,256,2048]{2,1,0:T(8,128)(2,1)}, u32[]{:S(2)}) copy-start(bf16[1,256,2048]{2,1,0:T(8,128)(2,1)} %stiffness.3) | copy-start | bytes 3145732
  25.7 10.8 %collective-permute-start.2 = (bf16[8,256,256]{2,1,0:T(8,128)(2,1)S(1)}, bf16[8,256,256]{2,1,0:T(8,128)(2,1)S(1)}, u32[]{:S(2)}, u32[]{:S(2)}) collective-permute-start(bf16[8,256,256]{2,1,0:T(8,128)(2,1)S(1)} %get-tuple-element.14.mine), channel_id=1, source_target_pairs={{0,1},{1,0},{2,3},{3,2},{4,5},{5,4},{6,7},{7,6},{8,9},{9,8},{10,11... | collective-permute-start | bytes 3145736 | tf_op jit(solution)/shard_map/ppermute | solution.py:174
